TPU v7x, 128 devices: a whole 4x4x4 slice. The times are simulated.
128 devices in a mesh: section: 4 (over z), tensor: 8 (over y_lo, x), dp: 4 (over y_hi, core).
Axes of the slice: x: 4, y: 4 (y_hi: 2, y_lo: 2; y = y_hi * 2 + y_lo), z: 4, core: 2. Of those that a mesh axis runs over, the one named last changes fastest.
Arguments:
- weights: bfloat16 [4, 8192, 8192], P('section', None, 'tensor'), may hold values from -0.0625 to 0.0625
- acts: bfloat16 [4, 4, 256, 8192], P('section', None, 'dp', 'tensor'), may hold values from -0.1875 to 0.1875
- gates: bfloat16 [4, 4, 256, 8192], P('section', None, 'dp', 'tensor'), may hold values from 0.25 to 1.75
- out_grad: bfloat16 [4, 256, 8192], P(None, 'dp', 'tensor'), may hold values from -6 to 6
- owner_rows: int32 [4, 4], replicated, may hold values from 8 to 24, as said below
Outputs:
- owned_grad: bfloat16 [4, 4, 3072, 8192], P('section', 'dp', None, 'tensor')
- section_grads: bfloat16 [4, 4, 256, 8192], P('section', None, 'dp', 'tensor')
Inputs may be any that keep to these rules, and one draw needn't show every extreme that they name: `owner_rows`: each row sums to 64; owners take consecutive row ranges in dp order; in every section one owner holds exactly the maximum, and the first owner holds fewer than 16 blocks.
All inputs are finite; a program needn't handle non-finite values.
Results may differ from a plain program's by a relative error of at most 0.035.
Values may be sent and summed in bfloat16 or wider, within the bound.
A program may use at most 448 MiB of HBM per device.

v0:
```python
import jax
import jax.numpy as jnp
from jax import lax
from jax.sharding import PartitionSpec as P

OWN_BLK = 128


def passed_along(block, axis, distance):
    devices = range(lax.axis_size(axis))
    route = [(i - distance, i) for i in devices if i - distance in devices]
    return lax.ppermute(block, axis, route)


def padded(cells, sides, width):
    for axis, dim in sides:
        count = lax.axis_size(axis)
        ends = count - 1
        head = lax.slice_in_dim(cells, 0, width, axis=dim)
        tail = lax.slice_in_dim(cells, cells.shape[dim] - width, cells.shape[dim], axis=dim)
        cells = jnp.concatenate(
            [
                lax.ppermute(tail, axis, [(i, (i + 1) % count) for i in range(ends)]),
                cells,
                lax.ppermute(head, axis, [((i + 1) % count, i) for i in range(ends)]),
            ],
            axis=dim,
        )
    return cells


def masked_rows(extended, start, count, cap):
    piece = lax.dynamic_slice_in_dim(extended, start, cap, 0)
    keep = jnp.arange(cap)[:, None] < count
    return jnp.where(keep, piece, jnp.zeros_like(piece))


def on_device(weights, acts, gates, out_grad, owner_rows):
    weight = weights[0]
    inputs_here = acts[0]
    gate_here = gates[0]
    micro_count, token_count, columns = inputs_here.shape
    width = weight.shape[0]
    section_count = lax.axis_size("section")
    section_index = lax.axis_index("section")
    owner_count = lax.axis_size("dp")
    cap = 3 * width // (2 * owner_count)
    is_last = section_index == section_count - 1
    incoming = jnp.zeros((token_count, columns), jnp.bfloat16)
    grads = jnp.zeros((micro_count, token_count, columns), jnp.bfloat16)
    saved_pre = jnp.zeros((micro_count, token_count, columns), jnp.bfloat16)
    for step_index in range(micro_count + section_count - 1):
        arrived = passed_along(incoming, "section", -1)
        micro = step_index - (section_count - 1 - section_index)
        valid = (micro >= 0) & (micro < micro_count)
        slot = jnp.clip(micro, 0, micro_count - 1)
        given = lax.dynamic_index_in_dim(out_grad, slot, 0, keepdims=False)
        upstream = jnp.where(is_last, given, arrived)
        gate_now = lax.dynamic_index_in_dim(gate_here, slot, 0, keepdims=False)
        pre_grad = (upstream.astype(jnp.float32) * gate_now.astype(jnp.float32)).astype(
            jnp.bfloat16
        )
        partial_value = lax.dot_general(
            pre_grad, weight, (((1,), (1,)), ((), ())), preferred_element_type=jnp.float32
        )
        summed = lax.psum_scatter(
            partial_value.astype(jnp.bfloat16), "tensor", scatter_dimension=1, tiled=True
        )
        grads = jnp.where(valid, lax.dynamic_update_index_in_dim(grads, summed, slot, 0), grads)
        saved_pre = jnp.where(
            valid, lax.dynamic_update_index_in_dim(saved_pre, pre_grad, slot, 0), saved_pre
        )
        incoming = summed
    owner_row = lax.dynamic_index_in_dim(owner_rows, section_index, 0, keepdims=False)
    counts = owner_row * OWN_BLK
    starts = jnp.cumsum(counts) - counts
    weight_partial = lax.dot_general(
        lax.all_gather(inputs_here, "tensor", axis=2, tiled=True),
        saved_pre,
        (((0, 1), (0, 1)), ((), ())),
        preferred_element_type=jnp.float32,
    )
    rounded = weight_partial.astype(jnp.bfloat16)
    shares = lax.psum_scatter(
        rounded.astype(jnp.float32).astype(jnp.bfloat16), "dp", scatter_dimension=0, tiled=True
    )
    share_rows = shares.shape[0]
    nearby = padded(shares, (("dp", 0),), share_rows)
    extended = jnp.concatenate([nearby, jnp.zeros((cap, columns), jnp.bfloat16)], axis=0)
    owner_index = lax.axis_index("dp")
    my_start = lax.dynamic_index_in_dim(starts, owner_index, 0, keepdims=False)
    my_count = lax.dynamic_index_in_dim(counts, owner_index, 0, keepdims=False)
    local_start = my_start - (owner_index - 1) * share_rows
    owned = masked_rows(extended, local_start, my_count, cap)
    return (owned[None, None], grads[None])


def solution(mesh):
    placed = (
        P("section", None, "tensor"),
        P("section", None, "dp", "tensor"),
        P("section", None, "dp", "tensor"),
        P(None, "dp", "tensor"),
        P(),
    )
    return jax.shard_map(
        on_device,
        mesh=mesh,
        in_specs=placed,
        out_specs=(P("section", "dp", None, "tensor"), P("section", None, "dp", "tensor")),
        check_vma=False,
    )
```

profile of v0, /device:TPU:1, one launch (start us, length us, event | category | flops | bytes accessed | tf_op | source)
XLA Modules:
  0.0 649.4 jit_solution(9829288021972385691)
XLA Ops:
  8.7 6.3 collective-permute-done
  16.1 11.9 %fusion.15 = bf16[64,8192]{1,0:T(8,128)(2,1)} fusion(bf16[64,1024]{1,0:T(8,128)(2,1)S(1)} %get-tuple-element.15, bf16[1,8192,1024]{2,1,0:T(8,128)(2,1)} %param.5), kind=kOutput, calls=%fused_computation.20 | convolution fusion | flops 1074266112 | bytes 17956864 | tf_op jit(solution)/shard_map/dot_general | solution.py:63
  28.1 36.9 %reduce-scatter.9.cloned.1.call-done = bf16[64,1024]{1,0:T(8,128)(2,1)} async-done(((bf16[64,8192]{1,0:T(8,128)(2,1)}), bf16[64,1024]{1,0:T(8,128)(2,1)}) %reduce-scatter.9.cloned.1.call-update) | async-done | bytes 131088 | tf_op jit(solution)/shard_map/reduce_scatter | solution.py:66
  66.3 4.6 collective-permute-done.1
  71.0 11.9 %fusion.18 = bf16[64,8192]{1,0:T(8,128)(2,1)} fusion(bf16[64,1024]{1,0:T(8,128)(2,1)S(1)} %get-tuple-element.13, bf16[1,8192,1024]{2,1,0:T(8,128)(2,1)} %param.5), kind=kOutput, calls=%fused_computation.21 | convolution fusion | flops 1074266112 | bytes 17956864 | tf_op jit(solution)/shard_map/dot_general | solution.py:63
  83.0 38.9 %reduce-scatter.11.cloned.1.call-done = bf16[64,1024]{1,0:T(8,128)(2,1)} async-done(((bf16[64,8192]{1,0:T(8,128)(2,1)}), bf16[64,1024]{1,0:T(8,128)(2,1)}) %reduce-scatter.11.cloned.1.call-update) | async-done | bytes 131088 | tf_op jit(solution)/shard_map/reduce_scatter | solution.py:66
  121.9 1.7 collective-permute-start.2
  123.7 4.2 collective-permute-done.2
  127.9 11.9 %fusion.21 = bf16[64,8192]{1,0:T(8,128)(2,1)} fusion(bf16[64,1024]{1,0:T(8,128)(2,1)S(1)} %get-tuple-element.11, bf16[1,8192,1024]{2,1,0:T(8,128)(2,1)} %param.5), kind=kOutput, calls=%fused_computation.22 | convolution fusion | flops 1074266112 | bytes 17956864 | tf_op jit(solution)/shard_map/dot_general | solution.py:63
  139.9 39.1 %reduce-scatter.13.cloned.1.call-done = bf16[64,1024]{1,0:T(8,128)(2,1)} async-done(((bf16[64,8192]{1,0:T(8,128)(2,1)}), bf16[64,1024]{1,0:T(8,128)(2,1)}) %reduce-scatter.13.cloned.1.call-update) | async-done | bytes 131088 | tf_op jit(solution)/shard_map/reduce_scatter | solution.py:66
  180.3 4.6 collective-permute-done.3
  185.0 11.9 %fusion.24 = bf16[64,8192]{1,0:T(8,128)(2,1)} fusion(bf16[64,1024]{1,0:T(8,128)(2,1)S(1)} %get-tuple-element.9, bf16[1,8192,1024]{2,1,0:T(8,128)(2,1)} %param.5), kind=kOutput, calls=%fused_computation.23 | convolution fusion | flops 1074266112 | bytes 17956864 | tf_op jit(solution)/shard_map/dot_general | solution.py:63
  197.0 39.1 %reduce-scatter.15.cloned.1.call-done = bf16[64,1024]{1,0:T(8,128)(2,1)} async-done(((bf16[64,8192]{1,0:T(8,128)(2,1)}), bf16[64,1024]{1,0:T(8,128)(2,1)}) %reduce-scatter.15.cloned.1.call-update) | async-done | bytes 131088 | tf_op jit(solution)/shard_map/reduce_scatter | solution.py:66
  236.1 1.5 collective-permute-start.4
  237.6 4.4 collective-permute-done.4
  242.1 11.9 %fusion.27 = bf16[64,8192]{1,0:T(8,128)(2,1)} fusion(bf16[64,1024]{1,0:T(8,128)(2,1)S(1)} %get-tuple-element.7, bf16[1,8192,1024]{2,1,0:T(8,128)(2,1)} %param.5), kind=kOutput, calls=%fused_computation.24 | convolution fusion | flops 1074266112 | bytes 17956864 | tf_op jit(solution)/shard_map/dot_general | solution.py:63
  254.1 39.1 %reduce-scatter.17.cloned.1.call-done = bf16[64,1024]{1,0:T(8,128)(2,1)} async-done(((bf16[64,8192]{1,0:T(8,128)(2,1)}), bf16[64,1024]{1,0:T(8,128)(2,1)}) %reduce-scatter.17.cloned.1.call-update) | async-done | bytes 131088 | tf_op jit(solution)/shard_map/reduce_scatter | solution.py:66
  294.5 4.6 collective-permute-done.5
  299.2 11.9 %fusion.30 = bf16[64,8192]{1,0:T(8,128)(2,1)} fusion(bf16[64,1024]{1,0:T(8,128)(2,1)S(1)} %get-tuple-element.5, bf16[1,8192,1024]{2,1,0:T(8,128)(2,1)} %param.5), kind=kOutput, calls=%fused_computation.25 | convolution fusion | flops 1074266112 | bytes 17956864 | tf_op jit(solution)/shard_map/dot_general | solution.py:63
  312.0 38.4 %reduce-scatter.19.cloned.1.call-done = bf16[64,1024]{1,0:T(8,128)(2,1)} async-done(((bf16[64,8192]{1,0:T(8,128)(2,1)}), bf16[64,1024]{1,0:T(8,128)(2,1)}) %reduce-scatter.19.cloned.1.call-update) | async-done | bytes 131088 | tf_op jit(solution)/shard_map/reduce_scatter | solution.py:66
  351.6 4.6 collective-permute-done.6
  356.3 52.1 %all-gather.3.cloned.1.call-done = bf16[1,4,64,8192]{3,2,1,0:T(8,128)(2,1)} async-done(((bf16[1,4,64,1024]{3,2,1,0:T(8,128)(2,1)}), bf16[1,4,64,8192]{3,2,1,0:T(8,128)(2,1)}) %all-gather.3.cloned.1.call-update) | async-done | bytes 4194320 | tf_op jit(solution)/shard_map/all_gather | solution.py:78
  408.4 10.3 %fusion.14 = bf16[8192,1024]{0,1:T(8,128)(2,1)} fusion(bf16[4,64,1024]{2,1,0:T(8,128)(2,1)S(1)} %get-tuple-element.2, bf16[1,4,64,8192]{3,2,1,0:T(8,128)(2,1)} %all-gather.3.cloned.1.call-done), kind=kOutput, calls=%fused_computation.19 | convolution fusion | flops 4303355904 | bytes 21495808 | tf_op jit(solution)/shard_map/dot_general | solution.py:77
  418.8 131.9 %reduce-scatter.21.cloned.1.call-done = bf16[2048,1024]{0,1:T(8,128)(2,1)} async-done(((bf16[8192,1024]{0,1:T(8,128)(2,1)}), bf16[2048,1024]{0,1:T(8,128)(2,1)}) %reduce-scatter.21.cloned.1.call-update) | async-done | bytes 4194320 | tf_op jit(solution)/shard_map/reduce_scatter | solution.py:84
  550.7 2.5 collective-permute-start.7
  553.2 4.1 collective-permute-start.8
  557.3 11.9 %fusion.33 = bf16[64,8192]{1,0:T(8,128)(2,1)} fusion(bf16[64,1024]{1,0:T(8,128)(2,1)S(1)} %get-tuple-element.3, bf16[1,8192,1024]{2,1,0:T(8,128)(2,1)} %param.5), kind=kOutput, calls=%fused_computation.26 | convolution fusion | flops 1074266112 | bytes 17956864 | tf_op jit(solution)/shard_map/dot_general | solution.py:63
  572.4 31.3 %reduce-scatter.23.cloned.1.call-done = bf16[64,1024]{1,0:T(8,128)(2,1)} async-done(((bf16[64,8192]{1,0:T(8,128)(2,1)}), bf16[64,1024]{1,0:T(8,128)(2,1)}) %reduce-scatter.23.cloned.1.call-update) | async-done | bytes 131088 | tf_op jit(solution)/shard_map/reduce_scatter | solution.py:66
  604.7 6.5 %copy.8 = bf16[2048,1024]{1,0:T(8,128)(2,1)} copy(bf16[2048,1024]{0,1:T(8,128)(2,1)} %reduce-scatter.21.cloned.1.call-done) | data formatting | bytes 8388608 | tf_op jit(solution)/shard_map/reduce_scatter | solution.py:84
  611.3 6.3 copy.7
  617.6 6.5 copy.9
  624.9 17.8 %fusion.40 = bf16[1,1,3072,1024]{3,2,1,0:T(8,128)(2,1)} fusion(bf16[3072,1024]{1,0:T(8,128)(2,1)S(1)} %broadcast.55, s32[]{:T(128)S(6)} %select_n.244, bf16[2048,1024]{1,0:T(8,128)(2,1)} %copy.7, bf16[2048,1024]{1,0:T(8,128)(2,1)} %copy.8, bf16[2048,1024]{1,0:T(8,128)(2,1)} %copy.9, pred[3072]{0:T(1024)(128)(4,1)S(1)} %iota_compare_fusion), kind=kLoop, calls=%fused_computation.31 | loop fusion | flops 28311552 | bytes 25168900 | tf_op jit(solution)/shard_map/broadcast_in_dim | solution.py:95
  (71 shorter events, 13.4 us)
Async XLA Ops:
  7.2 63.7 %copy-start = (bf16[1,4,64,1024]{3,2,1,0:T(8,128)(2,1)S(1)}, bf16[1,4,64,1024]{3,2,1,0:T(8,128)(2,1)}, u32[]{:S(2)}) copy-start(bf16[1,4,64,1024]{3,2,1,0:T(8,128)(2,1)} %param.7) | copy-start | bytes 1572868
  7.2 63.7 %copy-start.1 = (bf16[4,64,1024]{2,1,0:T(8,128)(2,1)S(1)}, bf16[4,64,1024]{2,1,0:T(8,128)(2,1)}, u32[]{:S(2)}) copy-start(bf16[4,64,1024]{2,1,0:T(8,128)(2,1)} %param.8) | copy-start | bytes 1572868
  7.2 57.8 %reduce-scatter.9.cloned.1.call-start = ((), (), s32[]{:S(2)}) async-start(), calls=%async_computation.8 | async-start | bytes 1179648 | tf_op jit(solution)/shard_map/reduce_scatter | solution.py:66
  7.3 7.7 %collective-permute-start = (bf16[64,1024]{1,0:T(8,128)(2,1)S(1)}, bf16[64,1024]{1,0:T(8,128)(2,1)S(1)}, u32[]{:S(2)}, u32[]{:S(2)}) collective-permute-start(bf16[64,1024]{1,0:T(8,128)(2,1)S(1)} %broadcast_in_dim.60), channel_id=1, source_target_pairs={{32,0},{64,32},{96,64},{33,1},{65,33},{97,65},{34,2},{66,34},{98,6... | collective-permute-start | bytes 393224 | tf_op jit(solution)/shard_map/ppermute | solution.py:12
  28.0 93.9 %reduce-scatter.11.cloned.1.call-start = ((), (), s32[]{:S(2)}) async-start(), calls=%async_computation.9 | async-start | bytes 1179648 | tf_op jit(solution)/shard_map/reduce_scatter | solution.py:66
  65.0 5.9 collective-permute-start.1
  83.0 96.1 %reduce-scatter.13.cloned.1.call-start = ((), (), s32[]{:S(2)}) async-start(), calls=%async_computation.10 | async-start | bytes 1179648 | tf_op jit(solution)/shard_map/reduce_scatter | solution.py:66
  121.9 5.9 collective-permute-start.2
  139.8 96.2 %reduce-scatter.15.cloned.1.call-start = ((), (), s32[]{:S(2)}) async-start(), calls=%async_computation.11 | async-start | bytes 1179648 | tf_op jit(solution)/shard_map/reduce_scatter | solution.py:66
  179.0 5.9 collective-permute-start.3
  197.0 96.2 %reduce-scatter.17.cloned.1.call-start = ((), (), s32[]{:S(2)}) async-start(), calls=%async_computation.12 | async-start | bytes 1179648 | tf_op jit(solution)/shard_map/reduce_scatter | solution.py:66
  236.1 5.9 collective-permute-start.4
  254.0 96.3 %reduce-scatter.19.cloned.1.call-start = ((), (), s32[]{:S(2)}) async-start(), calls=%async_computation.13 | async-start | bytes 1179648 | tf_op jit(solution)/shard_map/reduce_scatter | solution.py:66
  293.2 5.9 collective-permute-start.5
  311.2 97.2 %all-gather.3.cloned.1.call-start = ((), (), s32[]{:S(2)}) async-start(), calls=%async_computation.16 | async-start | bytes 4718592 | tf_op jit(solution)/shard_map/all_gather | solution.py:78
  311.9 238.8 %reduce-scatter.21.cloned.1.call-start = ((), (), s32[]{:S(2)}) async-start(), calls=%async_computation.14 | async-start | bytes 20971520 | tf_op jit(solution)/shard_map/reduce_scatter | solution.py:84
  350.3 5.9 collective-permute-start.6
  418.7 150.5 %copy-start.9 = (s32[4,4]{1,0:T(4,128)S(1)}, s32[4,4]{1,0:T(4,128)}, u32[]{:S(2)}) copy-start(s32[4,4]{1,0:T(4,128)} %param.9) | copy-start | bytes 196
  418.7 153.3 %copy-start.8 = (bf16[64,1024]{1,0:T(8,128)(2,1)S(1)}, bf16[64,1024]{1,0:T(8,128)(2,1)}, u32[]{:S(2)}) copy-start(bf16[64,1024]{1,0:T(8,128)(2,1)} %reduce-scatter.9.cloned.1.call-done) | copy-start | bytes 393220
  418.7 153.4 %copy-start.3 = (bf16[64,1024]{1,0:T(8,128)(2,1)S(1)}, bf16[64,1024]{1,0:T(8,128)(2,1)}, u32[]{:S(2)}) copy-start(bf16[64,1024]{1,0:T(8,128)(2,1)} %reduce-scatter.11.cloned.1.call-done) | copy-start | bytes 393220
  418.8 153.4 %copy-start.4 = (bf16[64,1024]{1,0:T(8,128)(2,1)S(1)}, bf16[64,1024]{1,0:T(8,128)(2,1)}, u32[]{:S(2)}) copy-start(bf16[64,1024]{1,0:T(8,128)(2,1)} %reduce-scatter.13.cloned.1.call-done) | copy-start | bytes 393220
  418.8 153.4 %copy-start.5 = (bf16[64,1024]{1,0:T(8,128)(2,1)S(1)}, bf16[64,1024]{1,0:T(8,128)(2,1)}, u32[]{:S(2)}) copy-start(bf16[64,1024]{1,0:T(8,128)(2,1)} %reduce-scatter.15.cloned.1.call-done) | copy-start | bytes 393220
  418.8 153.5 %copy-start.6 = (bf16[64,1024]{1,0:T(8,128)(2,1)S(1)}, bf16[64,1024]{1,0:T(8,128)(2,1)}, u32[]{:S(2)}) copy-start(bf16[64,1024]{1,0:T(8,128)(2,1)} %reduce-scatter.17.cloned.1.call-done) | copy-start | bytes 393220
  418.8 153.5 %copy-start.7 = (bf16[64,1024]{1,0:T(8,128)(2,1)S(1)}, bf16[64,1024]{1,0:T(8,128)(2,1)}, u32[]{:S(2)}) copy-start(bf16[64,1024]{1,0:T(8,128)(2,1)} %reduce-scatter.19.cloned.1.call-done) | copy-start | bytes 393220
  418.8 185.0 %reduce-scatter.23.cloned.1.call-start = ((), (), s32[]{:S(2)}) async-start(), calls=%async_computation.15 | async-start | bytes 1179648 | tf_op jit(solution)/shard_map/reduce_scatter | solution.py:66
  550.7 60.5 %collective-permute-start.7 = (bf16[2048,1024]{0,1:T(8,128)(2,1)}, bf16[2048,1024]{0,1:T(8,128)(2,1)}, u32[]{:S(2)}, u32[]{:S(2)}) collective-permute-start(bf16[2048,1024]{0,1:T(8,128)(2,1)} %reduce-scatter.21.cloned.1.call-done), channel_id=1, source_target_pairs={{0,1},{1,2},{2,3},{4,5},{5,6},{6,7},{8,9},{9,10},{10,11},{12,13},{... | collective-permute-start | bytes 12582920 | tf_op jit(solution)/shard_map/ppermute | solution.py:23
  553.2 64.4 %collective-permute-start.8 = (bf16[2048,1024]{0,1:T(8,128)(2,1)}, bf16[2048,1024]{0,1:T(8,128)(2,1)}, u32[]{:S(2)}, u32[]{:S(2)}) collective-permute-start(bf16[2048,1024]{0,1:T(8,128)(2,1)} %reduce-scatter.21.cloned.1.call-done), channel_id=1, source_target_pairs={{1,0},{2,1},{3,2},{5,4},{6,5},{7,6},{9,8},{10,9},{11,10},{13,12},{... | collective-permute-start | bytes 12582920 | tf_op jit(solution)/shard_map/ppermute | solution.py:25
  604.7 19.4 %copy-start.2 = (bf16[1,4,64,1024]{3,2,1,0:T(8,128)(2,1)}, bf16[1,4,64,1024]{3,2,1,0:T(8,128)(2,1)S(1)}, u32[]{:S(2)}) copy-start(bf16[1,4,64,1024]{3,2,1,0:T(8,128)(2,1)S(1)} %bitcast_dynamic-update-slice_fusion) | copy-start | bytes 1572868
Sparse Core Ops, SparseCore 0:
  28.1 36.8 reduce-scatter.8
  83.1 38.7 reduce-scatter.10
  140.0 38.9 reduce-scatter.12
  197.1 38.9 reduce-scatter.14
  254.2 38.9 reduce-scatter.16
  311.3 39.0 reduce-scatter.18
  352.0 56.3 all-gather.2
  418.8 131.8 reduce-scatter.20
  569.4 34.3 reduce-scatter.22
where the time goes:
time: 662 us; the launch traced here: 649 us
  waiting for transfers between devices  481 us (73%)
  matrix products  93.8 us (14%)
  local copies, waits for them, and re-layouts  21.5 us (3%)
  other arithmetic  21.3 us (3%)
  starting transfers between devices  16.6 us (3%)
  between operations  15.1 us (2%)
    reduce_scatter x7, waiting for transfers between devices, on_device(): lax.psum_scatter(partial_value.astype(jnp.bfloat16), 'tensor', scatter_di...  263 us
    reduce_scatter x1, waiting for transfers between devices, on_device(): lax.psum_scatter(rounded.astype(jnp.float32).astype(jnp.bfloat16), 'dp',...  132 us
    dot_general x7, matrix products, on_device(): lax.dot_general(pre_grad, weight, (((1,), (1,)), ((), ())), preferred_ele...  83.6 us
    all_gather x1, waiting for transfers between devices, on_device(): lax.all_gather(inputs_here, 'tensor', axis=2, tiled=True)  52.1 us
    ppermute x7, waiting for transfers between devices, passed_along(): return lax.ppermute(block, axis, route)  33.3 us
    broadcast_in_dim x1, other arithmetic, on_device(): return (owned[None, None], grads[None])  17.8 us
  transfers between devices with their start and end apart: 18, of which 16 were waited for; matrix products, arithmetic and copies ran while one was open for 4% of the time, Pallas kernels for 0%

commit v1 on v0

v1 whole, which is shorter than its diff:
```python
import functools

import jax
import jax.numpy as jnp
from jax import lax
from jax.experimental import pallas as pl
from jax.experimental.pallas import tpu as pltpu
from jax.sharding import PartitionSpec as P

OWN_BLK = 128
STEPS = 8
MESH = pl.DeviceIdType.MESH
BF = jnp.bfloat16
F32 = jnp.float32


def remote(src, dst, sems, index, device):
    return pltpu.make_async_remote_copy(
        src_ref=src,
        dst_ref=dst,
        send_sem=sems.at[(0,) + index],
        recv_sem=sems.at[(1,) + index],
        device_id=device,
        device_id_type=MESH,
    )


def pipeline_kernel(
    weight, acts, gates, out_grad,
    grads, all_acts, all_pre,
    wv, gv, ov, uv, pv, part, got_a, got_b, got_u, got_y, kept, total,
    w_sem, in_sem, og_sem, pre_sem, a_sem, b_sem, u_sem, y_sem, ag_sem, fix_sem, loc_sem, out_loc_sem, out_sem, g_sem, sib_sem,
):
    section = lax.axis_index("section")
    tensor = lax.axis_index("tensor")
    dp = lax.axis_index("dp")
    last_section = lax.axis_size("section") - 1
    x, yl = lax.rem(tensor, 4), tensor // 4
    yh, core = dp // 2, lax.rem(dp, 2)
    y = yh * 2 + yl
    micro = 256 // STEPS
    half = 512

    def at(x_, y_, z_, core_):
        y_ = lax.rem(y_ + 4, 4)
        return (z_, lax.rem(y_, 2) * 4 + lax.rem(x_ + 4, 4), (y_ // 2) * 2 + core_)

    right, left = at(x + 1, y, section, core), at(x - 1, y, section, core)
    up, down = at(x, y + 1, section, core), at(x, y - 1, section, core)
    across = at(x, y + 2, section, core)
    sibling = at(x, y, section, 1 - core)
    other_y = yh * 2 + 1 - yl
    partner = at(x, other_y, section, core)
    below = lax.rem(section + last_section, last_section + 1)
    above = lax.rem(section + 1, last_section + 1)
    below_same, below_other = at(x, y, below, core), at(x, other_y, below, core)
    above_same, above_other = at(x, y, above, core), at(x, other_y, above, core)

    mine = pl.ds(pl.multiple_of(core * half, half), half)
    theirs = pl.ds(pl.multiple_of((1 - core) * half, half), half)

    places = (
        (2, 0), (2, 1), (1, 1), (3, 0), (1, 0), (3, 1), (0, 1 - yl), (0, yl),
    )
    loads = []
    for k, (dx, l) in enumerate(places):
        start = (l * 4 + lax.rem(x + dx, 4)) * 1024 + core * half
        load = pltpu.make_async_copy(
            weight.at[pl.ds(pl.multiple_of(start, half), half), :], wv.at[k], w_sem.at[k]
        )
        load.start()
        loads.append(load)
    own_gate = pltpu.make_async_copy(gates.at[:, mine], gv.at[core], loc_sem.at[0])
    own_gate.start()
    own_acts = pltpu.make_async_copy(acts, all_acts.at[y, x, core], loc_sem.at[1])
    own_acts.start()
    own_grad = pltpu.make_async_copy(out_grad.at[:, mine], ov.at[core], loc_sem.at[2])

    barrier = pltpu.get_barrier_semaphore()
    neighbours = (
        right, left, up, down, across, sibling, below_same, below_other, above_same, above_other,
    )
    for device in neighbours:
        pl.semaphore_signal(barrier, inc=1, device_id=device, device_id_type=MESH)
    pl.semaphore_wait(barrier, len(neighbours))

    gate_swap = remote(gates.at[:, theirs], gv.at[core], in_sem, (), sibling)
    gate_swap.start()
    grad_swap = remote(out_grad.at[:, theirs], ov.at[core], og_sem, (), sibling)

    @pl.when(section == last_section)
    def _():
        own_grad.start()
        grad_swap.start()

    lo, hi = pl.ds(0, 128), pl.ds(128, 128)
    lo_a, lo_b = pl.ds(0, 64), pl.ds(64, 64)
    hi_a, hi_b = pl.ds(128, 64), pl.ds(192, 64)
    xr, xl = lax.rem(x + 1, 4), lax.rem(x + 3, 4)
    yu, yd = lax.rem(y + 1, 4), lax.rem(y + 3, 4)

    def copy(k, src, dst, device):
        return remote(src, dst, g_sem, (k,), device)

    def same(k, ref, device):
        return copy(k, ref, ref, device)

    def sib(k, ref):
        return remote(ref, ref, sib_sem, (k,), sibling)

    def phase1():
        t_lo, t_hi = all_acts.at[y, x, core, lo], all_acts.at[y, x, core, hi]
        return [
            copy(0, acts.at[lo], t_lo, right), copy(1, acts.at[lo], t_lo, left),
            copy(2, acts.at[hi], t_hi, up), copy(3, acts.at[hi], t_hi, down),
        ]

    def phase2():
        return [
            same(4, all_acts.at[y, xl, core, lo_a], right), same(5, all_acts.at[y, xr, core, lo_b], left),
            same(6, all_acts.at[yd, x, core, hi_a], up), same(7, all_acts.at[yu, x, core, hi_b], down),
        ]

    def phase3():
        row, column = all_acts.at[y, :, core, lo], all_acts.at[:, x, core, hi]
        return [same(8, row, up), same(9, row, down), same(10, column, right), same(11, column, left),
                sib(0, row), sib(1, column)]

    def phase4():
        return [
            same(12, all_acts.at[yd, :, core, lo_a], up), same(13, all_acts.at[yu, :, core, lo_b], down),
            same(14, all_acts.at[:, xl, core, hi_a], right), same(15, all_acts.at[:, xr, core, hi_b], left),
            sib(2, all_acts.at[yd, :, core, lo]), sib(3, all_acts.at[yu, :, core, lo]),
            sib(4, all_acts.at[:, xl, core, hi]), sib(5, all_acts.at[:, xr, core, hi]),
        ]

    def phase5():
        return [sib(6, all_acts.at[lax.rem(y + 2, 4), :, core, lo]), sib(7, all_acts.at[:, lax.rem(x + 2, 4), core, hi])]

    phases = (phase1, phase2, phase3, phase4, phase5)
    arrivals = (4, 4, 4, 4, 0)
    early = (1, 1, 2, 3, 9)

    def run_phase(index):
        if index == 2:
            own_acts.wait()
        if index > 0:
            for c in phases[index - 1]()[: arrivals[index - 1]]:
                c.wait_recv()
        for c in phases[index]():
            c.start()

    def gather(before):
        for index in range(len(phases)):
            first = last_section - section >= early[index]
            pl.when(first if before else jnp.logical_not(first))(functools.partial(run_phase, index))

    gather(True)

    own_gate.wait()
    gate_swap.wait()

    @pl.when(section == last_section)
    def _():
        own_grad.wait()
        grad_swap.wait()

    def rows_of(m):
        return pl.ds(pl.multiple_of(m * micro, micro), micro)

    def pre_swap(m):
        ref = pv.at[:, rows_of(m), mine]
        return remote(ref, ref, pre_sem, (m,), sibling)

    def pre_across(m):
        return remote(pv.at[:, rows_of(m), mine], all_pre.at[yh, :, rows_of(m), mine], ag_sem, (m,), across)

    def send_a(m, k):
        return remote(part.at[m, k], got_a.at[m, k], a_sem, (m, k), (right, left)[k])

    def send_b(m, k):
        return remote(part.at[m, 2 + k], got_b.at[m, k], b_sem, (m, k), (right, left)[k % 2])

    def send_u(m, k):
        return remote((kept.at[m], part.at[m, 6])[k], got_u.at[m, k], u_sem, (m, k), (below_same, below_other)[k])

    def send_y(m):
        return remote(part.at[m, 6], got_y.at[m], y_sem, (m,), partner)

    def grad_own(m):
        return pltpu.make_async_copy(total.at[core, rows_of(m), :], grads.at[rows_of(m), mine], out_loc_sem.at[m])

    def grad_other(m):
        return remote(total.at[1 - core, rows_of(m), :], grads.at[rows_of(m), mine], out_sem, (m,), sibling)

    def product(m, k):
        pre = jnp.concatenate([pv[0, rows_of(m), :], pv[1, rows_of(m), :]], axis=0)
        w = wv[2 * k : 2 * k + 2].reshape(2 * half, 1024)
        value = lax.dot_general(pre, w, (((1,), (1,)), ((), ())), preferred_element_type=F32).astype(BF)
        part[m, 2 * k] = value[:, :half]
        part[m, 2 * k + 1] = value[:, half:]

    def add3(m, role, l):
        return (
            part[m, role].astype(F32) + got_b[m, 1 - l].astype(F32) + got_b[m, 2 + l].astype(F32)
        ).astype(BF)

    def reduce_step(m):
        for k in range(4):
            send_b(m, k).wait_recv()
        part[m, 6] = add3(m, 6, 1 - yl)

        @pl.when(section > 0)
        def _():
            send_u(m, 1).start()

        send_y(m).start()
        kept[m] = add3(m, 7, yl)

        @pl.when(section > 0)
        def _():
            send_u(m, 0).start()

    def finish_step(m):
        send_y(m).wait_recv()
        value = (kept[m].astype(F32) + got_y[m].astype(F32)).astype(BF)
        total[0, rows_of(m), :] = value[:micro]
        total[1, rows_of(m), :] = value[micro:]
        grad_own(m).start()
        grad_other(m).start()

    def step(m, _):
        @pl.when(section == last_section)
        def _():
            uv[...] = ov[:, rows_of(m), :]

        @pl.when(section < last_section)
        def _():
            send_u(m, 0).wait_recv()
            send_u(m, 1).wait_recv()
            value = (got_u[m, 0].astype(F32) + got_u[m, 1].astype(F32)).astype(BF)
            uv[0] = value[:micro]
            uv[1] = value[micro:]

        pre = (uv[...].astype(F32) * gv[:, rows_of(m), :].astype(F32)).astype(BF)
        pv[:, rows_of(m), mine] = pre
        pre_swap(m).start()
        pre_across(m).start()

        @pl.when(m > 1)
        def _():
            finish_step(m - 2)

        @pl.when(m == 0)
        def _():
            loads[0].wait()
            loads[1].wait()

        pre_swap(m).wait_recv()
        product(m, 0)
        send_a(m, 0).start()
        send_a(m, 1).start()

        @pl.when(m == 0)
        def _():
            loads[2].wait()
            loads[3].wait()

        product(m, 1)
        send_b(m, 0).start()
        send_b(m, 1).start()

        @pl.when(m > 0)
        def _():
            reduce_step(m - 1)

        @pl.when(m == 0)
        def _():
            for k in range(4, 8):
                loads[k].wait()

        product(m, 2)
        for k in range(2):
            send_a(m, k).wait_recv()
            part[m, 4 + k] = (part[m, 4 + k].astype(F32) + got_a[m, k].astype(F32)).astype(BF)
            send_b(m, 2 + k).start()
        product(m, 3)
        return 0

    lax.fori_loop(0, STEPS, step, 0)
    reduce_step(STEPS - 1)
    keep_pre = pltpu.make_async_copy(pv, all_pre.at[yh], loc_sem.at[3])
    keep_pre.start()
    gather(False)
    for m in range(STEPS):
        pre_across(m).wait_recv()
    fix = remote(all_pre.at[1 - yh, :, :, mine], all_pre.at[1 - yh, :, :, mine], fix_sem, (), sibling)
    fix.start()
    finish_step(STEPS - 2)
    finish_step(STEPS - 1)

    def drain(m, _):
        pre_swap(m).wait_send()
        pre_across(m).wait_send()
        for k in range(2):
            send_a(m, k).wait_send()
        for k in range(4):
            send_b(m, k).wait_send()

        @pl.when(section > 0)
        def _():
            send_u(m, 0).wait_send()
            send_u(m, 1).wait_send()

        send_y(m).wait_send()
        grad_own(m).wait()
        grad_other(m).wait()
        return 0

    lax.fori_loop(0, STEPS, drain, 0)
    for index, phase in enumerate(phases):
        for k, c in enumerate(phase()):
            c.wait_send()
            if k >= arrivals[index]:
                c.wait_recv()
    keep_pre.wait()
    fix.wait()


def run_pipeline(weight, acts, gates, out_grad):
    width = weight.shape[0]
    dma = pltpu.SemaphoreType.DMA
    micro = 2 * 256 // STEPS
    return pl.pallas_call(
        pipeline_kernel,
        out_shape=(
            jax.ShapeDtypeStruct((256, 1024), BF),
            jax.ShapeDtypeStruct((4, 4, 2, 256, 1024), BF),
            jax.ShapeDtypeStruct((2, 2, 256, 1024), BF),
        ),
        in_specs=[pl.BlockSpec(memory_space=pl.ANY)] * 4,
        out_specs=(pl.BlockSpec(memory_space=pl.ANY),) * 3,
        scratch_shapes=[
            pltpu.VMEM((8, 512, 1024), BF),
            pltpu.VMEM((2, 256, 512), BF),
            pltpu.VMEM((2, 256, 512), BF),
            pltpu.VMEM((2, micro // 2, 512), BF),
            pltpu.VMEM((2, 256, 1024), BF),
            pltpu.VMEM((STEPS, 8, micro, 512), BF),
            pltpu.VMEM((STEPS, 2, micro, 512), BF),
            pltpu.VMEM((STEPS, 4, micro, 512), BF),
            pltpu.VMEM((STEPS, 2, micro, 512), BF),
            pltpu.VMEM((STEPS, micro, 512), BF),
            pltpu.VMEM((STEPS, micro, 512), BF),
            pltpu.VMEM((2, 256, 512), BF),
            dma((8,)),
            dma((2,)),
            dma((2,)),
            dma((2, STEPS)),
            dma((2, STEPS, 2)),
            dma((2, STEPS, 4)),
            dma((2, STEPS, 2)),
            dma((2, STEPS)),
            dma((2, STEPS)),
            dma((2,)),
            dma((4,)),
            dma((STEPS,)),
            dma((2, STEPS)),
            dma((2, 16)),
            dma((2, 8)),
        ],
        compiler_params=pltpu.CompilerParams(
            collective_id=0, has_side_effects=True, vmem_limit_bytes=40 * 2**20
        ),
        cost_estimate=pl.CostEstimate(
            flops=2 * 512 * 1024 * width // 2, bytes_accessed=2 * width * 1024, transcendentals=0
        ),
        name="pipeline",
    )(weight, acts, gates, out_grad)


def owned_kernel(meta, a0, a1, a2, a3, pre, out):
    i = pl.program_id(0)
    rhs = pre[...].reshape(1024, 1024)
    lhs = jnp.concatenate([a[...].reshape(1024, 128) for a in (a0, a1, a2, a3)], axis=1)
    value = lax.dot_general(lhs, rhs, (((0,), (0,)), ((), ())), preferred_element_type=F32).astype(BF)
    for k in range(4):
        rows = value[k * 128 : (k + 1) * 128]
        out[k * 128 : (k + 1) * 128, :] = jnp.where(4 * i + k < meta[1], rows, jnp.zeros_like(rows))


def run_owned(meta, all_acts, all_pre, cap):
    def place(k):
        def index(i, meta):
            block = jnp.minimum(meta[0] + jnp.minimum(4 * i + k, meta[1] - 1), 63)
            return (0, block // 32, (block // 8) % 4, 0, 0, block % 8)

        return pl.BlockSpec((2, 1, 1, 2, 256, 128), index)

    view = all_acts.reshape(2, 2, 4, 2, 256, 1024)
    return pl.pallas_call(
        owned_kernel,
        out_shape=jax.ShapeDtypeStruct((cap, 1024), BF),
        grid_spec=pltpu.PrefetchScalarGridSpec(
            num_scalar_prefetch=1,
            grid=(cap // 512,),
            in_specs=[place(k) for k in range(4)] + [pl.BlockSpec((2, 2, 256, 1024), lambda i, meta: (0, 0, 0, 0))],
            out_specs=pl.BlockSpec((512, 1024), lambda i, meta: (i, 0)),
        ),
        compiler_params=pltpu.CompilerParams(vmem_limit_bytes=40 * 2**20),
        cost_estimate=pl.CostEstimate(
            flops=2 * cap * 1024 * 1024, bytes_accessed=2 * (2 * cap * 1024 + 1024 * 1024), transcendentals=0
        ),
        name="owned",
    )(meta, view, view, view, view, all_pre)


def on_device(weights, acts, gates, out_grad, owner_rows):
    width = weights.shape[1]
    cap = 3 * width // (2 * lax.axis_size("dp"))
    tokens = acts.shape[1] * acts.shape[2]
    flat = lambda a: a.reshape(tokens, a.shape[-1])
    grads, all_acts, all_pre = run_pipeline(weights[0], flat(acts[0]), flat(gates[0]), flat(out_grad))
    counts = lax.dynamic_index_in_dim(owner_rows, lax.axis_index("section"), 0, keepdims=False)
    owner = lax.axis_index("dp")
    start = jnp.sum(jnp.where(jnp.arange(counts.shape[0]) < owner, counts, 0))
    count = lax.dynamic_index_in_dim(counts, owner, 0, keepdims=False)
    owned = run_owned(jnp.stack([start, count]).astype(jnp.int32), all_acts, all_pre, cap)
    return owned[None, None], grads.reshape(acts.shape)


def solution(mesh):
    placed = (
        P("section", None, "tensor"),
        P("section", None, "dp", "tensor"),
        P("section", None, "dp", "tensor"),
        P(None, "dp", "tensor"),
        P(),
    )
    return jax.shard_map(
        on_device,
        mesh=mesh,
        in_specs=placed,
        out_specs=(P("section", "dp", None, "tensor"), P("section", None, "dp", "tensor")),
        check_vma=False,
    )
```

time: 662 us -> 146 us (0.22)
  the two profiles are of different devices: /device:TPU:1 before, /device:TPU:81 now
where the time goes in v1:
time: 146 us
  Pallas kernels  137 us (94%)
  local copies, waits for them, and re-layouts  5.19 us (4%)
  other arithmetic  2.69 us (2%)
    pallas_call x1, Pallas kernels, run_pipeline(): pl.pallas_call(pipeline_kernel, out_shape=(jax.ShapeDtypeStruct((256, 102...  126 us
    pallas_call x1, Pallas kernels, run_owned(): pl.pallas_call(owned_kernel, out_shape=jax.ShapeDtypeStruct((cap, 1024),...  11.9 us
    unnamed x7, local copies, waits for them, and re-layouts  3.92 us

profile of v1, /device:TPU:81, one launch (start us, length us, event | category | flops | bytes accessed | tf_op | source)
XLA Modules:
  0.0 146.0 jit_solution(13455144674577648525)
XLA Ops:
  0.6 1.3 dynamic_slice.11
  1.9 1.3 fusion
  3.2 1.4 pad_add_fusion.meta
  4.6 0.0 copy-start
  4.6 1.0 copy-done
  5.6 0.0 copy-start.1
  5.6 1.0 copy-done.1
  6.7 0.0 copy-start.2
  6.7 1.0 copy-done.2
  7.7 125.6 %pipeline.1 = (bf16[256,1024]{1,0:T(8,128)(2,1)S(1)}, bf16[4,4,2,256,1024]{4,3,2,1,0:T(8,128)(2,1)}, bf16[2,2,256,1024]{3,2,1,0:T(8,128)(2,1)S(1)}) custom-call(bf16[8192,1024]{1,0:T(8,128)(2,1)} %bitcast.19, bf16[256,1024]{1,0:T(8,128)(2,1)S(1)} %bitcast.11, bf16[256,1024]{1,0:T(8,128)(2,1)S(1)} %bitcast.12, bf16[256,1024]{1,0:T(8,128)(2,1)S(1)} %bitcast.13), custom_call_target="tpu_custom_call" | custom-call | flops 4294967296 | bytes 16777216 | tf_op jit(solution)/shard_map/pipeline/pallas_call | solution.py:334
  133.3 11.9 %owned.1 = bf16[3072,1024]{1,0:T(8,128)(2,1)} custom-call(s32[2]{0:T(128)S(1)} %pad_add_fusion.meta, bf16[2,2,4,2,256,1024]{5,4,3,2,1,0:T(8,128)(2,1)} %bitcast.15, bf16[2,2,4,2,256,1024]{5,4,3,2,1,0:T(8,128)(2,1)} %bitcast.16, bf16[2,2,4,2,256,1024]{5,4,3,2,1,0:T(8,128)(2,1)} %bitcast.17, bf16[2,2,4,2,256,1024]{5,4,3,2,1,0:T(8,128)(2,1)} %bitcast.18, ...), custom_call_target="tpu_custom_call" | custom-call | flops 6442450944 | bytes 14680064 | tf_op jit(solution)/shard_map/owned/pallas_call | solution.py:401
  145.2 0.8 copy.8
Async XLA Ops:
  4.6 1.0 copy-start
  5.6 1.0 copy-start.1
  6.7 1.0 copy-start.2

commit v2 on v1

v2 whole, which is shorter than its diff:
```python
import jax
import jax.numpy as jnp
from jax import lax
from jax.experimental import pallas as pl
from jax.experimental.pallas import tpu as pltpu
from jax.sharding import PartitionSpec as P

OWN_BLK = 128
BLOCKS = 4
STEPS = 8
MESH = pl.DeviceIdType.MESH
BF = jnp.bfloat16
F32 = jnp.float32


def remote(src, dst, sems, index, device):
    return pltpu.make_async_remote_copy(
        src_ref=src,
        dst_ref=dst,
        send_sem=sems.at[(0,) + index],
        recv_sem=sems.at[(1,) + index],
        device_id=device,
        device_id_type=MESH,
    )


def each(count, body):
    def wrapped(i, _):
        body(i)
        return 0

    lax.fori_loop(0, count, wrapped, 0)


def window_kernel(
    weight, acts, gates, out_grad,
    grads, av, pav,
    own, wv, wt, gv, ov, part, got_a, got_b, got_u, got_y, kept, total, sums,
    w_sem, gate_sem, og_sem, pre_sem, a_sem, b_sem, u_sem, y_sem, ag_sem, fix_sem, loc_sem,
    out_loc_sem, out_sem, back_sem, paced_sem, g_sem, sib_sem,
):
    section = lax.axis_index("section")
    tensor = lax.axis_index("tensor")
    dp = lax.axis_index("dp")
    last_section = lax.axis_size("section") - 1
    x, yl = lax.rem(tensor, 4), tensor // 4
    yh, core = dp // 2, lax.rem(dp, 2)
    y = yh * 2 + yl
    tokens, width = gates.shape
    micro = tokens // STEPS
    half = width // 2
    is_last = section == last_section
    is_first = section == 0

    def at(x_, y_, z_, core_):
        y_ = lax.rem(y_ + 4, 4)
        return (z_, lax.rem(y_, 2) * 4 + lax.rem(x_ + 4, 4), (y_ // 2) * 2 + core_)

    right, left = at(x + 1, y, section, core), at(x - 1, y, section, core)
    up, down = at(x, y + 1, section, core), at(x, y - 1, section, core)
    across = at(x, y + 2, section, core)
    sibling = at(x, y, section, 1 - core)
    other_y = yh * 2 + 1 - yl
    partner = at(x, other_y, section, core)
    diagonal = at(x - 1 + 2 * yl, other_y, section, core)
    below = lax.rem(section + last_section, last_section + 1)
    above = lax.rem(section + 1, last_section + 1)
    below_same, below_other = at(x, y, below, core), at(x, other_y, below, core)
    above_same, above_other = at(x, y, above, core), at(x, other_y, above, core)
    below_sibling, above_sibling = at(x, y, below, 1 - core), at(x, y, above, 1 - core)

    mine = pl.ds(pl.multiple_of(core * half, half), half)
    theirs = pl.ds(pl.multiple_of((1 - core) * half, half), half)

    own_gate = pltpu.make_async_copy(gates.at[:, mine], gv.at[core], loc_sem.at[0])
    own_gate.start()
    own_grad = pltpu.make_async_copy(out_grad.at[:, mine], ov.at[core], loc_sem.at[2])
    pl.when(is_last)(own_grad.start)

    places = (
        (2, 0), (2, 1), (1, 1), (3, 0), (1, 0), (3, 1), (0, 1 - yl), (0, yl),
    )
    loads = []
    for k, (dx, l) in enumerate(places):
        start = (l * 4 + lax.rem(x + dx, 4)) * 1024 + core * half
        load = pltpu.make_async_copy(
            weight.at[pl.ds(pl.multiple_of(start, half), half), :], wv.at[k], w_sem.at[k]
        )
        load.start()
        loads.append(load)
    own_acts = pltpu.make_async_copy(acts, own, loc_sem.at[1])
    keep_own = pltpu.make_async_copy(own, av.at[yh, yl, x, core], loc_sem.at[3])
    own_acts.start()

    barrier = pltpu.get_barrier_semaphore()
    neighbours = (
        right, left, up, down, across, diagonal, sibling, below_same, below_other, below_sibling,
        above_same, above_other, above_sibling,
    )
    for device in neighbours:
        pl.semaphore_signal(barrier, inc=1, device_id=device, device_id_type=MESH)

    def turn(k):
        for j in range(2):
            loads[2 * k + j].wait()
            wt[k, :, j * half : (j + 1) * half] = wv[2 * k + j].T

    turn(0)
    turn(1)
    pl.semaphore_wait(barrier, len(neighbours))

    gate_swap = remote(gates.at[:, theirs], gv.at[core], gate_sem, (), sibling)
    gate_swap.start()
    grad_swap = remote(out_grad.at[:, theirs], ov.at[core], og_sem, (), sibling)
    pl.when(is_last)(grad_swap.start)

    tok = tokens // 2
    lo, hi = pl.ds(0, tok), pl.ds(tok, tok)
    lo_a, lo_b = pl.ds(0, tok // 2), pl.ds(tok // 2, tok // 2)
    hi_a, hi_b = pl.ds(tok, tok // 2), pl.ds(tok + tok // 2, tok // 2)
    xr, xl, x2 = lax.rem(x + 1, 4), lax.rem(x + 3, 4), lax.rem(x + 2, 4)
    yu, yd, y2 = lax.rem(y + 1, 4), lax.rem(y + 3, 4), lax.rem(y + 2, 4)
    piece = tok // STEPS

    def tile(y_, x_, rows=None):
        ref = av.at[y_ // 2, lax.rem(y_, 2), x_, core]
        return ref if rows is None else ref.at[rows]

    def same(k, ref, device):
        return remote(ref, ref, g_sem, (k,), device)

    def sib(k, ref):
        return remote(own if k == 0 else ref, ref, sib_sem, (k,), sibling)

    def paced(which, q, y_lo, x_lo, y_hi, x_hi, to_lo, to_hi):
        rows_lo = pl.ds(pl.multiple_of(q * piece, piece), piece)
        rows_hi = pl.ds(pl.multiple_of(tok + q * piece, piece), piece)
        ref_lo, ref_hi = tile(y_lo, x_lo, rows_lo), tile(y_hi, x_hi, rows_hi)
        src_lo, src_hi = (own.at[rows_lo], own.at[rows_hi]) if which == 0 else (ref_lo, ref_hi)
        return [
            remote(src, ref, paced_sem, (which, q, k), device)
            for k, (src, ref, device) in enumerate(
                [
                    (src_lo, ref_lo, to_lo[0]), (src_lo, ref_lo, to_lo[1]),
                    (src_hi, ref_hi, to_hi[0]), (src_hi, ref_hi, to_hi[1]),
                ]
            )
        ]

    def set_a(q):
        return paced(0, q, y, x, y, x, (right, left), (up, down))

    def set_c(q):
        return paced(1, q, y, xl, yd, x, (up, down), (right, left))

    def set_b():
        return [
            remote(own.at[rows], tile(y, x, rows), g_sem, (k,), device)
            for k, (rows, device) in enumerate([(lo, up), (lo, down), (hi, right), (hi, left)])
        ]

    def set_f():
        return [
            same(4, tile(y, xl, lo_a), right), same(5, tile(y, xr, lo_b), left),
            same(6, tile(yd, x, hi_a), up), same(7, tile(yu, x, hi_b), down),
        ]

    def set_d():
        right_lo, up_hi = tile(y, xr, lo), tile(yu, x, hi)
        return [same(8, right_lo, up), same(9, right_lo, down), same(10, up_hi, right), same(11, up_hi, left)]

    def set_e(q):
        return paced(2, q, y, x2, y2, x, (up, down), (right, left))

    def set_g():
        return [
            same(16, tile(yd, xl, lo_a), up), same(17, tile(yu, xl, lo_b), down),
            same(18, tile(yd, xr, lo_a), up), same(19, tile(yu, xr, lo_b), down),
            same(20, tile(yd, x, lo_a), up), same(21, tile(yu, x, lo_b), down),
            same(22, tile(yd, xl, hi_a), right), same(23, tile(yd, xr, hi_b), left),
            same(24, tile(yu, xl, hi_a), right), same(25, tile(yu, xr, hi_b), left),
            same(26, tile(y, xl, hi_a), right), same(27, tile(y, xr, hi_b), left),
        ]

    def set_h():
        return [
            same(28, tile(yd, x2, lo_a), up), same(29, tile(yu, x2, lo_b), down),
            same(30, tile(y2, xl, hi_a), right), same(31, tile(y2, xr, hi_b), left),
        ]

    tiles = (
        (y, x),
        (y, xl), (y, xr), (yd, x), (yu, x), (yd, xl), (yd, xr), (yu, xl), (yu, xr),
        (y, x2), (y2, x), (yd, x2), (yu, x2), (y2, xl), (y2, xr),
        (y2, x2),
    )

    def sibs(first, end):
        return [sib(k, tile(*tiles[k])) for k in range(first, end)]

    def start(copies):
        for c in copies:
            c.start()

    def arrived(copies):
        for c in copies:
            c.wait_recv()

    def gather_second():
        start(set_f())

    def gather_third():
        each(STEPS, lambda q: start(set_c(q)))
        start(set_d())

    def gather_fourth():
        arrived(set_b())

        @pl.when(section != last_section - 2)
        def _():
            arrived(set_f())
            each(STEPS, lambda q: start(set_e(q)))

        each(STEPS, lambda q: arrived(set_c(q)))
        arrived(set_d())
        start(set_g())
        start(sibs(1, 9))

    def gather_fifth():
        each(STEPS, lambda q: arrived(set_e(q)))
        arrived(set_g())
        start(set_h())
        start(sibs(9, 15))

    def gather_sixth():
        arrived(set_h())
        start(sibs(15, 16))

    turn(2)
    turn(3)
    own_acts.wait()
    keep_own.start()

    @pl.when(section < last_section)
    def _():
        each(STEPS, lambda q: start(set_a(q)))
        start(set_b())
        start(sibs(0, 1))
        each(STEPS, lambda q: arrived(set_a(q)))
        start(set_f())

    @pl.when(section < last_section - 1)
    def _():
        gather_third()

    pl.when(section == last_section - 2)(lambda: arrived(set_f()))
    pl.when(is_first)(gather_fourth)

    own_gate.wait()
    gate_swap.wait()

    @pl.when(is_last)
    def _():
        own_grad.wait()
        grad_swap.wait()

    def rows_of(m):
        return pl.ds(pl.multiple_of(m * micro, micro), micro)

    def pre_swap(m):
        ref = pav.at[yh, :, rows_of(m), mine]
        return remote(ref, ref, pre_sem, (m,), sibling)

    def pre_across(m):
        ref = pav.at[yh, :, rows_of(m), mine]
        return remote(ref, ref, ag_sem, (m,), across)

    def send_a(m, k):
        return remote(part.at[m, k], got_a.at[m, k], a_sem, (m, k), (right, left)[k])

    def send_b(m, k):
        return remote(part.at[m, 2 + k], got_b.at[m, k], b_sem, (m, k), (right, left)[k])

    def send_same(m):
        return remote(part.at[m, 4 + yl], got_b.at[m, 2], b_sem, (m, 2), at(x + 1 - 2 * yl, y, section, core))

    def send_diagonal(m):
        return remote(part.at[m, 5 - yl], got_b.at[m, 3], b_sem, (m, 3), diagonal)

    def send_u(m, k):
        return remote((kept.at[m], part.at[m, 6])[k], got_u.at[m, k], u_sem, (m, k), (below_same, below_other)[k])

    def send_y(m):
        return remote(part.at[m, 6], got_y.at[m], y_sem, (m,), partner)

    def send_back(m, k):
        src = sums.at[(core, 1 - core)[k], rows_of(m), :]
        return remote(src, grads.at[rows_of(m), mine], back_sem, (m, k), (above_same, above_sibling)[k])

    def grad_own(m):
        return pltpu.make_async_copy(total.at[core, rows_of(m), :], grads.at[rows_of(m), mine], out_loc_sem.at[m])

    def grad_other(m):
        return remote(total.at[1 - core, rows_of(m), :], grads.at[rows_of(m), mine], out_sem, (m,), sibling)

    def product(m, k):
        pre = jnp.concatenate([pav[yh, 0, rows_of(m), :], pav[yh, 1, rows_of(m), :]], axis=0)
        value = jnp.dot(pre, wt[k], preferred_element_type=F32).astype(BF)
        part[m, 2 * k] = value[:, :half]
        part[m, 2 * k + 1] = value[:, half:]

    def forward_step(m):
        for k in range(2):
            send_a(m, k).wait_recv()
            part[m, 4 + k] = (part[m, 4 + k].astype(F32) + got_a[m, k].astype(F32)).astype(BF)
        send_diagonal(m).start()
        send_same(m).start()

    def partner_step(m):
        for k in range(2):
            send_b(m, k).wait_recv()
        part[m, 6] = (part[m, 6].astype(F32) + got_b[m, yl].astype(F32)).astype(BF)

        @pl.when(section > 0)
        def _():
            send_u(m, 1).start()

        @pl.when(is_first)
        def _():
            send_y(m).start()

    def reduce_step(m):
        send_same(m).wait_recv()
        send_diagonal(m).wait_recv()
        kept[m] = (
            (part[m, 7].astype(F32) + got_b[m, 1 - yl].astype(F32))
            + (got_b[m, 2].astype(F32) + got_b[m, 3].astype(F32))
        ).astype(BF)

        @pl.when(section > 0)
        def _():
            send_u(m, 0).start()

    def finish_step(m):
        send_y(m).wait_recv()
        value = (kept[m].astype(F32) + got_y[m].astype(F32)).astype(BF)
        total[0, rows_of(m), :] = value[:micro]
        total[1, rows_of(m), :] = value[micro:]
        grad_own(m).start()
        grad_other(m).start()

    def times_gate(m, upstream):
        pre = (upstream.astype(F32) * gv[:, rows_of(m), :].astype(F32)).astype(BF)
        pav[yh, :, rows_of(m), mine] = pre
        pre_swap(m).start()

    def take_step(m):
        @pl.when(is_last)
        def _():
            times_gate(m, ov[:, rows_of(m), :])

        @pl.when(section < last_section)
        def _():
            send_u(m, 0).wait_recv()
            send_u(m, 1).wait_recv()
            value = (got_u[m, 0].astype(F32) + got_u[m, 1].astype(F32)).astype(BF).reshape(2, micro, half)
            times_gate(m, value)
            sums[:, rows_of(m), :] = value

    def give_back(m):
        @pl.when(section < last_section)
        def _():
            for k in range(2):
                send_back(m, k).start()

    def paced_gather(m):
        pl.when(is_last)(lambda: start(set_a(m)))
        pl.when(section == last_section - 1)(lambda: start(set_c(m)))
        pl.when(section == last_section - 2)(lambda: start(set_e(m)))

    def step(m):
        take_step(m)
        pre_across(m).start()
        give_back(m)
        pre_swap(m).wait_recv()
        product(m, 0)
        send_a(m, 0).start()
        send_a(m, 1).start()


        @pl.when(m > 0)
        def _():
            product(m - 1, 2)
            forward_step(m - 1)


        @pl.when(m > 1)
        def _():
            reduce_step(m - 2)


        @pl.when(m > 0)
        def _():
            product(m - 1, 3)

        product(m, 1)
        send_b(m, 0).start()
        send_b(m, 1).start()


        @pl.when(m > 0)
        def _():
            partner_step(m - 1)

        paced_gather(m)


        @pl.when(m > 2)
        def _():
            pl.when(is_first)(lambda: finish_step(m - 3))

        pl.when(is_first & (m == 2))(gather_fifth)
        pl.when(is_first & (m == 4))(gather_sixth)

    fix_ref = pav.at[1 - yh, :, :, mine]
    fix = remote(fix_ref, fix_ref, fix_sem, (), sibling)

    def exchange_pre():
        each(STEPS, lambda m: pre_across(m).wait_recv())
        fix.start()
        fix.wait_recv()

    each(STEPS, step)
    product(STEPS - 1, 2)
    forward_step(STEPS - 1)
    reduce_step(STEPS - 2)
    product(STEPS - 1, 3)
    partner_step(STEPS - 1)

    @pl.when(is_first)
    def _():
        exchange_pre()
        arrived(sibs(0, 16))

    reduce_step(STEPS - 1)

    @pl.when(is_last)
    def _():
        start(set_b())
        start(sibs(0, 1))
        each(STEPS, lambda q: arrived(set_a(q)))
        start(set_f())
        gather_third()

    @pl.when(section == last_section - 1)
    def _():
        start(set_d())

    @pl.when(section > 0)
    def _():
        exchange_pre()
        gather_fourth()
        gather_fifth()
        gather_sixth()
        arrived(sibs(0, 16))

    @pl.when(is_first)
    def _():
        finish_step(STEPS - 3)
        finish_step(STEPS - 2)
        finish_step(STEPS - 1)

    def drain(m):
        pre_swap(m).wait_send()
        pre_across(m).wait_send()
        for k in range(2):
            send_a(m, k).wait_send()
        for k in range(2):
            send_b(m, k).wait_send()
        send_same(m).wait_send()
        send_diagonal(m).wait_send()
        for c in set_a(m) + set_c(m) + set_e(m):
            c.wait_send()

        @pl.when(section > 0)
        def _():
            for k in range(2):
                send_u(m, k).wait_send()
                send_back(m, k).wait_recv()

        @pl.when(section < last_section)
        def _():
            for k in range(2):
                send_back(m, k).wait_send()

        @pl.when(is_first)
        def _():
            send_y(m).wait_send()
            grad_own(m).wait()
            grad_other(m).wait()

    each(STEPS, drain)
    for c in set_b() + set_f() + set_d() + set_g() + set_h() + sibs(0, 16):
        c.wait_send()
    fix.wait_send()
    keep_own.wait()


def run_window(weight, acts, gates, out_grad):
    tokens, width = acts.shape
    rows = weight.shape[0]
    half = width // 2
    dma = pltpu.SemaphoreType.DMA
    micro = 2 * tokens // STEPS
    hbm = pl.BlockSpec(memory_space=pl.ANY)
    return pl.pallas_call(
        window_kernel,
        out_shape=(
            pltpu.VMEM((tokens, width), BF),
            jax.ShapeDtypeStruct((2, 2, 4, 2, tokens, width), BF),
            pltpu.VMEM((2, 2, tokens, width), BF),
        ),
        in_specs=[hbm] * 4,
        out_specs=(pl.BlockSpec(memory_space=pltpu.VMEM), hbm, pl.BlockSpec(memory_space=pltpu.VMEM)),
        scratch_shapes=[
            pltpu.VMEM((tokens, width), BF),
            pltpu.VMEM((8, half, width), BF),
            pltpu.VMEM((4, width, width), BF),
            pltpu.VMEM((2, tokens, half), BF),
            pltpu.VMEM((2, tokens, half), BF),
            pltpu.VMEM((STEPS, 8, micro, half), BF),
            pltpu.VMEM((STEPS, 2, micro, half), BF),
            pltpu.VMEM((STEPS, 4, micro, half), BF),
            pltpu.VMEM((STEPS, 2, micro, half), BF),
            pltpu.VMEM((STEPS, micro, half), BF),
            pltpu.VMEM((STEPS, micro, half), BF),
            pltpu.VMEM((2, tokens, half), BF),
            pltpu.VMEM((2, tokens, half), BF),
            dma((8,)),
            dma((2,)),
            dma((2,)),
            dma((2, STEPS)),
            dma((2, STEPS, 2)),
            dma((2, STEPS, 4)),
            dma((2, STEPS, 2)),
            dma((2, STEPS)),
            dma((2, STEPS)),
            dma((2,)),
            dma((4,)),
            dma((STEPS,)),
            dma((2, STEPS)),
            dma((2, STEPS, 2)),
            dma((2, 3, STEPS, 4)),
            dma((2, 32)),
            dma((2, 16)),
        ],
        compiler_params=pltpu.CompilerParams(
            collective_id=0, has_side_effects=True, vmem_limit_bytes=60 * 2**20
        ),
        cost_estimate=pl.CostEstimate(
            flops=2 * tokens * width * rows,
            bytes_accessed=2 * rows * width,
            transcendentals=0,
        ),
        name="window",
    )(weight, acts, gates, out_grad)


def owned_kernel(owners, acts, pre, owned, held, stage, in_sem, out_sem):
    section, owner = lax.axis_index("section"), lax.axis_index("dp")
    tokens, width = pre.shape[2:]
    first = jnp.int32(0)
    for k in range(3):
        first = first + jnp.where(k < owner, owners[section, k], 0)
    count = owners[section, owner]
    blocks = held.shape[0]
    group = BLOCKS
    rows = group * OWN_BLK

    def load(b):
        block = jnp.clip(first + jnp.minimum(b, count - 1), 0, 63)
        lane = pl.ds(pl.multiple_of(lax.rem(block, 8) * OWN_BLK, OWN_BLK), OWN_BLK)
        src = acts.at[:, lax.div(block, 32), lax.rem(lax.div(block, 8), 4), :, :, lane]
        return pltpu.make_async_copy(src, held.at[b], in_sem.at[b])

    def out(i):
        part = pl.ds(pl.multiple_of(i * rows, rows), rows)
        return pltpu.make_async_copy(stage.at[part], owned.at[part], out_sem.at[i])

    def chunk(i):
        for k in range(group):
            load(group * i + k).wait()
        lhs = jnp.concatenate(
            [held[group * i + k].reshape(4 * tokens, OWN_BLK) for k in range(group)], axis=1
        )
        rhs = pre[...].reshape(4 * tokens, width)
        value = lax.dot_general(lhs, rhs, (((0,), (0,)), ((), ())), preferred_element_type=F32).astype(BF)
        for k in range(group):
            piece = value[k * OWN_BLK : (k + 1) * OWN_BLK]
            stage[pl.ds(pl.multiple_of(i * rows + k * OWN_BLK, OWN_BLK), OWN_BLK), :] = jnp.where(
                group * i + k < count, piece, jnp.zeros_like(piece)
            )
        out(i).start()

    each(blocks, lambda b: load(b).start())
    each(blocks // group, chunk)
    each(blocks // group, lambda i: out(i).wait())


def run_owned(owners, acts, pre, cap):
    tokens, width = pre.shape[2:]
    hbm = pl.BlockSpec(memory_space=pl.ANY)
    blocks = cap // OWN_BLK
    return pl.pallas_call(
        owned_kernel,
        out_shape=jax.ShapeDtypeStruct((cap, width), BF),
        in_specs=[pl.BlockSpec(memory_space=pltpu.SMEM), hbm, pl.BlockSpec(memory_space=pltpu.VMEM)],
        out_specs=hbm,
        scratch_shapes=[
            pltpu.VMEM((blocks, 2, 2, tokens, OWN_BLK), BF),
            pltpu.VMEM((cap, width), BF),
            pltpu.SemaphoreType.DMA((blocks,)),
            pltpu.SemaphoreType.DMA((blocks // BLOCKS,)),
        ],
        compiler_params=pltpu.CompilerParams(vmem_limit_bytes=40 * 2**20),
        cost_estimate=pl.CostEstimate(
            flops=8 * cap * width * tokens, bytes_accessed=12 * cap * width, transcendentals=0
        ),
        name="owned",
    )(owners, acts, pre)


def on_device(weights, acts, gates, out_grad, owner_rows):
    width = weights.shape[1]
    cap = 3 * width // (2 * lax.axis_size("dp"))
    tokens = acts.shape[1] * acts.shape[2]

    def flat(a):
        return a.reshape(tokens, a.shape[-1])

    grads, av, pav = run_window(weights[0], flat(acts[0]), flat(gates[0]), flat(out_grad))
    owned = run_owned(owner_rows, av, pav, cap)
    return owned[None, None], grads.reshape(acts.shape)


def solution(mesh):
    placed = (
        P("section", None, "tensor"),
        P("section", None, "dp", "tensor"),
        P("section", None, "dp", "tensor"),
        P(None, "dp", "tensor"),
        P(),
    )
    return jax.shard_map(
        on_device,
        mesh=mesh,
        in_specs=placed,
        out_specs=(P("section", "dp", None, "tensor"), P("section", None, "dp", "tensor")),
        check_vma=False,
    )
```

time: 146 us -> 123 us (0.84)
  the two profiles are of different devices: /device:TPU:81 before, /device:TPU:1 now
where the time goes in v2:
time: 123 us; the launch traced here: 122 us
  Pallas kernels  120 us (98%)
    pallas_call x1, Pallas kernels, run_window(): pl.pallas_call(window_kernel, out_shape=(pltpu.VMEM((tokens, width), BF),...  109 us
    pallas_call x1, Pallas kernels, run_owned(): pl.pallas_call(owned_kernel, out_shape=jax.ShapeDtypeStruct((cap, width),...  10.8 us

profile of v2, /device:TPU:1, one launch (start us, length us, event | category | flops | bytes accessed | tf_op | source)
XLA Modules:
  0.0 121.7 jit_solution(3700034451383846462)
XLA Ops:
  0.6 0.0 copy-start
  0.6 109.5 %window.1 = (bf16[256,1024]{1,0:T(8,128)(2,1)S(1)}, bf16[2,2,4,2,256,1024]{5,4,3,2,1,0:T(8,128)(2,1)}, bf16[2,2,256,1024]{3,2,1,0:T(8,128)(2,1)S(1)}) custom-call(bf16[8192,1024]{1,0:T(8,128)(2,1)} %bitcast.7, bf16[256,1024]{1,0:T(8,128)(2,1)} %bitcast.9, bf16[256,1024]{1,0:T(8,128)(2,1)} %bitcast.10, bf16[256,1024]{1,0:T(8,128)(2,1)} %bitcast.11), custom_call_target="tpu_custom_call" | custom-call | flops 4294967296 | bytes 16777216 | tf_op jit(solution)/shard_map/window/pallas_call | solution.py:516
  110.1 0.0 copy-done
  110.1 10.8 %owned.1 = bf16[3072,1024]{1,0:T(8,128)(2,1)} custom-call(s32[4,4]{1,0:T(4,128)S(1)} %copy-done, bf16[2,2,4,2,256,1024]{5,4,3,2,1,0:T(8,128)(2,1)} %get-tuple-element.5.acts, bf16[2,2,256,1024]{3,2,1,0:T(8,128)(2,1)S(1)} %get-tuple-element.6.pre), custom_call_target="tpu_custom_call" | custom-call | flops 6442450944 | bytes 37748736 | tf_op jit(solution)/shard_map/owned/pallas_call | solution.py:614
  120.9 0.8 copy.8
Async XLA Ops:
  0.6 109.5 %copy-start = (s32[4,4]{1,0:T(4,128)S(1)}, s32[4,4]{1,0:T(4,128)}, u32[]{:S(2)}) copy-start(s32[4,4]{1,0:T(4,128)} %owners.1) | copy-start | bytes 196

commit v3 on v2

--- a/solution.py
+++ b/solution.py
@@ -106,7 +106,6 @@
             wt[k, :, j * half : (j + 1) * half] = wv[2 * k + j].T
 
     turn(0)
-    turn(1)
     pl.semaphore_wait(barrier, len(neighbours))
 
     gate_swap = remote(gates.at[:, theirs], gv.at[core], gate_sem, (), sibling)
@@ -195,8 +194,25 @@
         (y2, x2),
     )
 
-    def sibs(first, end):
-        return [sib(k, tile(*tiles[k])) for k in range(first, end)]
+    def owned_there(k, core_):
+        y_, x_ = tiles[k]
+        t = lax.rem(y_, 2) * 4 + x_
+        owner = 2 * yh + core_
+        lowest = jnp.where(owner == 0, 0, jnp.where(owner == 1, 1, jnp.where(owner == 2, 2, 5)))
+        highest = jnp.where(owner == 0, 1, jnp.where(owner == 1, 4, jnp.where(owner == 2, 6, 7)))
+        return (t >= lowest) & (t <= highest)
+
+    def start_sibs(first, end):
+        for k in range(first, end):
+            pl.when(owned_there(k, 1 - core))(sib(k, tile(*tiles[k])).start)
+
+    def arrived_sibs():
+        for k in range(16):
+            pl.when(owned_there(k, core))(sib(k, tile(*tiles[k])).wait_recv)
+
+    def sent_sibs():
+        for k in range(16):
+            pl.when(owned_there(k, 1 - core))(sib(k, tile(*tiles[k])).wait_send)
 
     def start(copies):
         for c in copies:
@@ -224,20 +240,19 @@
         each(STEPS, lambda q: arrived(set_c(q)))
         arrived(set_d())
         start(set_g())
-        start(sibs(1, 9))
+        start_sibs(1, 9)
 
     def gather_fifth():
         each(STEPS, lambda q: arrived(set_e(q)))
         arrived(set_g())
         start(set_h())
-        start(sibs(9, 15))
+        start_sibs(9, 15)
 
     def gather_sixth():
         arrived(set_h())
-        start(sibs(15, 16))
-
-    turn(2)
-    turn(3)
+        start_sibs(15, 16)
+
+    turn(1)
     own_acts.wait()
     keep_own.start()
 
@@ -245,7 +260,7 @@
     def _():
         each(STEPS, lambda q: start(set_a(q)))
         start(set_b())
-        start(sibs(0, 1))
+        start_sibs(0, 1)
         each(STEPS, lambda q: arrived(set_a(q)))
         start(set_f())
 
@@ -253,8 +268,21 @@
     def _():
         gather_third()
 
-    pl.when(section == last_section - 2)(lambda: arrived(set_f()))
-    pl.when(is_first)(gather_fourth)
+    @pl.when(section == last_section - 2)
+    def _():
+        arrived(set_f())
+        each(STEPS, lambda q: start(set_e(q)))
+
+    @pl.when(is_first)
+    def _():
+        gather_fourth()
+        gather_fifth()
+
+
+    @pl.when(section < last_section)
+    def _():
+        turn(2)
+        turn(3)
 
     own_gate.wait()
     gate_swap.wait()
@@ -372,11 +400,6 @@
         def _():
             for k in range(2):
                 send_back(m, k).start()
-
-    def paced_gather(m):
-        pl.when(is_last)(lambda: start(set_a(m)))
-        pl.when(section == last_section - 1)(lambda: start(set_c(m)))
-        pl.when(section == last_section - 2)(lambda: start(set_e(m)))
 
     def step(m):
         take_step(m)
@@ -412,15 +435,18 @@
         def _():
             partner_step(m - 1)
 
-        paced_gather(m)
-
 
         @pl.when(m > 2)
         def _():
             pl.when(is_first)(lambda: finish_step(m - 3))
 
-        pl.when(is_first & (m == 2))(gather_fifth)
-        pl.when(is_first & (m == 4))(gather_sixth)
+        pl.when(is_first & (m == 2))(gather_sixth)
+
+        @pl.when(is_last & (m == 0))
+        def _():
+            turn(2)
+            turn(3)
+
 
     fix_ref = pav.at[1 - yh, :, :, mine]
     fix = remote(fix_ref, fix_ref, fix_sem, (), sibling)
@@ -440,21 +466,22 @@
     @pl.when(is_first)
     def _():
         exchange_pre()
-        arrived(sibs(0, 16))
+        arrived_sibs()
 
     reduce_step(STEPS - 1)
 
     @pl.when(is_last)
     def _():
+        each(STEPS, lambda q: start(set_a(q)))
         start(set_b())
-        start(sibs(0, 1))
+        start_sibs(0, 1)
         each(STEPS, lambda q: arrived(set_a(q)))
         start(set_f())
         gather_third()
 
     @pl.when(section == last_section - 1)
     def _():
-        start(set_d())
+        gather_third()
 
     @pl.when(section > 0)
     def _():
@@ -462,7 +489,7 @@
         gather_fourth()
         gather_fifth()
         gather_sixth()
-        arrived(sibs(0, 16))
+        arrived_sibs()
 
     @pl.when(is_first)
     def _():
@@ -500,8 +527,9 @@
             grad_other(m).wait()
 
     each(STEPS, drain)
-    for c in set_b() + set_f() + set_d() + set_g() + set_h() + sibs(0, 16):
+    for c in set_b() + set_f() + set_d() + set_g() + set_h():
         c.wait_send()
+    sent_sibs()
     fix.wait_send()
     keep_own.wait()
 
@@ -566,7 +594,7 @@
     )(weight, acts, gates, out_grad)
 
 
-def owned_kernel(owners, acts, pre, owned, held, stage, in_sem, out_sem):
+def owned_kernel(owners, acts, pre, grads, owned, grads_out, held, stage, in_sem, out_sem, copy_sem):
     section, owner = lax.axis_index("section"), lax.axis_index("dp")
     tokens, width = pre.shape[2:]
     first = jnp.int32(0)
@@ -603,31 +631,35 @@
         out(i).start()
 
     each(blocks, lambda b: load(b).start())
+    keep = pltpu.make_async_copy(grads, grads_out, copy_sem)
+    keep.start()
     each(blocks // group, chunk)
     each(blocks // group, lambda i: out(i).wait())
-
-
-def run_owned(owners, acts, pre, cap):
+    keep.wait()
+
+
+def run_owned(owners, acts, pre, grads, cap):
     tokens, width = pre.shape[2:]
     hbm = pl.BlockSpec(memory_space=pl.ANY)
     blocks = cap // OWN_BLK
     return pl.pallas_call(
         owned_kernel,
-        out_shape=jax.ShapeDtypeStruct((cap, width), BF),
-        in_specs=[pl.BlockSpec(memory_space=pltpu.SMEM), hbm, pl.BlockSpec(memory_space=pltpu.VMEM)],
-        out_specs=hbm,
+        out_shape=(jax.ShapeDtypeStruct((cap, width), BF), jax.ShapeDtypeStruct(grads.shape, BF)),
+        in_specs=[pl.BlockSpec(memory_space=pltpu.SMEM), hbm] + [pl.BlockSpec(memory_space=pltpu.VMEM)] * 2,
+        out_specs=(hbm, hbm),
         scratch_shapes=[
             pltpu.VMEM((blocks, 2, 2, tokens, OWN_BLK), BF),
             pltpu.VMEM((cap, width), BF),
             pltpu.SemaphoreType.DMA((blocks,)),
             pltpu.SemaphoreType.DMA((blocks // BLOCKS,)),
+            pltpu.SemaphoreType.DMA,
         ],
         compiler_params=pltpu.CompilerParams(vmem_limit_bytes=40 * 2**20),
         cost_estimate=pl.CostEstimate(
             flops=8 * cap * width * tokens, bytes_accessed=12 * cap * width, transcendentals=0
         ),
         name="owned",
-    )(owners, acts, pre)
+    )(owners, acts, pre, grads)
 
 
 def on_device(weights, acts, gates, out_grad, owner_rows):
@@ -639,7 +671,7 @@
         return a.reshape(tokens, a.shape[-1])
 
     grads, av, pav = run_window(weights[0], flat(acts[0]), flat(gates[0]), flat(out_grad))
-    owned = run_owned(owner_rows, av, pav, cap)
+    owned, grads = run_owned(owner_rows, av, pav, grads, cap)
     return owned[None, None], grads.reshape(acts.shape)
 
 

time: 123 us -> 116 us (0.943)
  Pallas kernels: 120 us -> 113 us
    pallas_call x1, Pallas kernels: 109 us -> 103 us  [run_window(): pl.pallas_call(window_kernel, out_shape=(pltpu.VMEM((tokens, width), BF),...]
where the time goes in v3:
time: 116 us; the launch traced here: 114 us
  Pallas kernels  113 us (97%)
    pallas_call x1, Pallas kernels, run_window(): pl.pallas_call(window_kernel, out_shape=(pltpu.VMEM((tokens, width), BF),...  103 us
    pallas_call x1, Pallas kernels, run_owned(): pl.pallas_call(owned_kernel, out_shape=(jax.ShapeDtypeStruct((cap, width)...  10.8 us

profile of v3, /device:TPU:1, one launch (start us, length us, event | category | flops | bytes accessed | tf_op | source)
XLA Modules:
  0.0 114.0 jit_solution(7205817064254417000)
XLA Ops:
  0.6 0.0 copy-start
  0.6 102.6 %window.1 = (bf16[256,1024]{1,0:T(8,128)(2,1)S(1)}, bf16[2,2,4,2,256,1024]{5,4,3,2,1,0:T(8,128)(2,1)}, bf16[2,2,256,1024]{3,2,1,0:T(8,128)(2,1)S(1)}) custom-call(bf16[8192,1024]{1,0:T(8,128)(2,1)} %bitcast.6, bf16[256,1024]{1,0:T(8,128)(2,1)} %bitcast.7, bf16[256,1024]{1,0:T(8,128)(2,1)} %bitcast.8, bf16[256,1024]{1,0:T(8,128)(2,1)} %bitcast.9), custom_call_target="tpu_custom_call" | custom-call | flops 4294967296 | bytes 16777216 | tf_op jit(solution)/shard_map/window/pallas_call | solution.py:544
  103.2 0.0 copy-done
  103.2 10.8 %owned.1 = (bf16[3072,1024]{1,0:T(8,128)(2,1)}, bf16[256,1024]{1,0:T(8,128)(2,1)}) custom-call(s32[4,4]{1,0:T(4,128)S(1)} %copy-done, bf16[2,2,4,2,256,1024]{5,4,3,2,1,0:T(8,128)(2,1)} %get-tuple-element.7.acts, bf16[2,2,256,1024]{3,2,1,0:T(8,128)(2,1)S(1)} %get-tuple-element.8.pre, bf16[256,1024]{1,0:T(8,128)(2,1)S(1)} %get-tuple-element.9.grads), custom_call_target="tpu_custom_call" | custom-call | flops 6442450944 | bytes 37748736 | tf_op jit(solution)/shard_map/owned/pallas_call | solution.py:645
Async XLA Ops:
  0.6 102.6 %copy-start = (s32[4,4]{1,0:T(4,128)S(1)}, s32[4,4]{1,0:T(4,128)}, u32[]{:S(2)}) copy-start(s32[4,4]{1,0:T(4,128)} %owners.1) | copy-start | bytes 196

commit v4 on v3

--- a/solution.py
+++ b/solution.py
@@ -108,10 +108,17 @@
     turn(0)
     pl.semaphore_wait(barrier, len(neighbours))
 
-    gate_swap = remote(gates.at[:, theirs], gv.at[core], gate_sem, (), sibling)
-    gate_swap.start()
-    grad_swap = remote(out_grad.at[:, theirs], ov.at[core], og_sem, (), sibling)
-    pl.when(is_last)(grad_swap.start)
+    first_rows, later_rows = pl.ds(0, micro), pl.ds(micro, tokens - micro)
+
+    def swap(src, dst, sems, k, rows):
+        return remote(src.at[rows, theirs], dst.at[core, rows], sems, (k,), sibling)
+
+    gate_swaps = [swap(gates, gv, gate_sem, k, rows) for k, rows in enumerate((first_rows, later_rows))]
+    grad_swaps = [swap(out_grad, ov, og_sem, k, rows) for k, rows in enumerate((first_rows, later_rows))]
+    gate_swaps[0].start()
+    pl.when(is_last)(grad_swaps[0].start)
+    gate_swaps[1].start()
+    pl.when(is_last)(grad_swaps[1].start)
 
     tok = tokens // 2
     lo, hi = pl.ds(0, tok), pl.ds(tok, tok)
@@ -285,12 +292,12 @@
         turn(3)
 
     own_gate.wait()
-    gate_swap.wait()
+    gate_swaps[0].wait()
 
     @pl.when(is_last)
     def _():
         own_grad.wait()
-        grad_swap.wait()
+        grad_swaps[0].wait()
 
     def rows_of(m):
         return pl.ds(pl.multiple_of(m * micro, micro), micro)
@@ -338,10 +345,14 @@
         part[m, 2 * k + 1] = value[:, half:]
 
     def forward_step(m):
-        for k in range(2):
-            send_a(m, k).wait_recv()
+        def merge(k):
             part[m, 4 + k] = (part[m, 4 + k].astype(F32) + got_a[m, k].astype(F32)).astype(BF)
+
+        send_a(m, 0).wait_recv()
+        send_a(m, 1).wait_recv()
+        merge(1 - yl)
         send_diagonal(m).start()
+        merge(yl)
         send_same(m).start()
 
     def partner_step(m):
@@ -442,6 +453,11 @@
 
         pl.when(is_first & (m == 2))(gather_sixth)
 
+        @pl.when(m == 0)
+        def _():
+            gate_swaps[1].wait()
+            pl.when(is_last)(grad_swaps[1].wait)
+
         @pl.when(is_last & (m == 0))
         def _():
             turn(2)
@@ -485,10 +501,12 @@
 
     @pl.when(section > 0)
     def _():
-        exchange_pre()
         gather_fourth()
+        each(STEPS, lambda m: pre_across(m).wait_recv())
+        fix.start()
         gather_fifth()
         gather_sixth()
+        fix.wait_recv()
         arrived_sibs()
 
     @pl.when(is_first)
@@ -565,8 +583,8 @@
             pltpu.VMEM((2, tokens, half), BF),
             pltpu.VMEM((2, tokens, half), BF),
             dma((8,)),
-            dma((2,)),
-            dma((2,)),
+            dma((2, 2)),
+            dma((2, 2)),
             dma((2, STEPS)),
             dma((2, STEPS, 2)),
             dma((2, STEPS, 4)),

time: 116 us -> 114 us (0.983); the launches traced: 114 us -> 114 us
  no operation moved by 1% of the time
where the time goes in v4:
time: 114 us
  Pallas kernels  114 us (100%)
    pallas_call x1, Pallas kernels, run_window(): pl.pallas_call(window_kernel, out_shape=(pltpu.VMEM((tokens, width), BF),...  103 us
    pallas_call x1, Pallas kernels, run_owned(): pl.pallas_call(owned_kernel, out_shape=(jax.ShapeDtypeStruct((cap, width)...  10.8 us

profile of v4, /device:TPU:1, one launch (start us, length us, event | category | flops | bytes accessed | tf_op | source)
XLA Modules:
  0.0 114.3 jit_solution(6605154522216607984)
XLA Ops:
  0.6 0.0 copy-start
  0.6 102.9 %window.1 = (bf16[256,1024]{1,0:T(8,128)(2,1)S(1)}, bf16[2,2,4,2,256,1024]{5,4,3,2,1,0:T(8,128)(2,1)}, bf16[2,2,256,1024]{3,2,1,0:T(8,128)(2,1)S(1)}) custom-call(bf16[8192,1024]{1,0:T(8,128)(2,1)} %bitcast.6, bf16[256,1024]{1,0:T(8,128)(2,1)} %bitcast.7, bf16[256,1024]{1,0:T(8,128)(2,1)} %bitcast.8, bf16[256,1024]{1,0:T(8,128)(2,1)} %bitcast.9), custom_call_target="tpu_custom_call" | custom-call | flops 4294967296 | bytes 16777216 | tf_op jit(solution)/shard_map/window/pallas_call | solution.py:562
  103.5 0.0 copy-done
  103.5 10.8 %owned.1 = (bf16[3072,1024]{1,0:T(8,128)(2,1)}, bf16[256,1024]{1,0:T(8,128)(2,1)}) custom-call(s32[4,4]{1,0:T(4,128)S(1)} %copy-done, bf16[2,2,4,2,256,1024]{5,4,3,2,1,0:T(8,128)(2,1)} %get-tuple-element.7.acts, bf16[2,2,256,1024]{3,2,1,0:T(8,128)(2,1)S(1)} %get-tuple-element.8.pre, bf16[256,1024]{1,0:T(8,128)(2,1)S(1)} %get-tuple-element.9.grads), custom_call_target="tpu_custom_call" | custom-call | flops 6442450944 | bytes 37748736 | tf_op jit(solution)/shard_map/owned/pallas_call | solution.py:663
Async XLA Ops:
  0.6 102.9 %copy-start = (s32[4,4]{1,0:T(4,128)S(1)}, s32[4,4]{1,0:T(4,128)}, u32[]{:S(2)}) copy-start(s32[4,4]{1,0:T(4,128)} %owners.1) | copy-start | bytes 196

commit v5 on v4

--- a/solution.py
+++ b/solution.py
@@ -421,27 +421,21 @@
         send_a(m, 0).start()
         send_a(m, 1).start()
 
-
         @pl.when(m > 0)
         def _():
             product(m - 1, 2)
             forward_step(m - 1)
+            product(m - 1, 3)
 
 
         @pl.when(m > 1)
         def _():
             reduce_step(m - 2)
-
-
-        @pl.when(m > 0)
-        def _():
-            product(m - 1, 3)
 
         product(m, 1)
         send_b(m, 0).start()
         send_b(m, 1).start()
 
-
         @pl.when(m > 0)
         def _():
             partner_step(m - 1)
@@ -470,21 +464,70 @@
     def exchange_pre():
         each(STEPS, lambda m: pre_across(m).wait_recv())
         fix.start()
-        fix.wait_recv()
+
+    def drain_step(m):
+        pre_swap(m).wait_send()
+        pre_across(m).wait_send()
+        for k in range(2):
+            send_a(m, k).wait_send()
+            send_b(m, k).wait_send()
+        send_same(m).wait_send()
+        send_diagonal(m).wait_send()
+
+        @pl.when(section > 0)
+        def _():
+            for k in range(2):
+                send_u(m, k).wait_send()
+                send_back(m, k).wait_recv()
+
+        @pl.when(section < last_section)
+        def _():
+            for k in range(2):
+                send_back(m, k).wait_send()
+
+        @pl.when(is_first)
+        def _():
+            send_y(m).wait_send()
+            grad_own(m).wait()
+            grad_other(m).wait()
+
+    def drain_gather():
+        def paced_out(q):
+            for c in set_a(q) + set_c(q) + set_e(q):
+                c.wait_send()
+
+        each(STEPS, paced_out)
+        for c in set_b() + set_f() + set_d() + set_g():
+            c.wait_send()
+        keep_own.wait()
+
+    def drain_last():
+        for c in set_h():
+            c.wait_send()
+        sent_sibs()
 
     each(STEPS, step)
     product(STEPS - 1, 2)
     forward_step(STEPS - 1)
+    product(STEPS - 1, 3)
     reduce_step(STEPS - 2)
-    product(STEPS - 1, 3)
     partner_step(STEPS - 1)
 
     @pl.when(is_first)
     def _():
         exchange_pre()
+        finish_step(STEPS - 3)
+        finish_step(STEPS - 2)
         arrived_sibs()
+        drain_gather()
+        drain_last()
+        each(STEPS - 1, drain_step)
 
     reduce_step(STEPS - 1)
+
+    @pl.when(is_first)
+    def _():
+        finish_step(STEPS - 1)
 
     @pl.when(is_last)
     def _():
@@ -502,54 +545,16 @@
     @pl.when(section > 0)
     def _():
         gather_fourth()
-        each(STEPS, lambda m: pre_across(m).wait_recv())
-        fix.start()
+        exchange_pre()
+        each(STEPS - 1, drain_step)
         gather_fifth()
+        drain_gather()
         gather_sixth()
-        fix.wait_recv()
         arrived_sibs()
-
-    @pl.when(is_first)
-    def _():
-        finish_step(STEPS - 3)
-        finish_step(STEPS - 2)
-        finish_step(STEPS - 1)
-
-    def drain(m):
-        pre_swap(m).wait_send()
-        pre_across(m).wait_send()
-        for k in range(2):
-            send_a(m, k).wait_send()
-        for k in range(2):
-            send_b(m, k).wait_send()
-        send_same(m).wait_send()
-        send_diagonal(m).wait_send()
-        for c in set_a(m) + set_c(m) + set_e(m):
-            c.wait_send()
-
-        @pl.when(section > 0)
-        def _():
-            for k in range(2):
-                send_u(m, k).wait_send()
-                send_back(m, k).wait_recv()
-
-        @pl.when(section < last_section)
-        def _():
-            for k in range(2):
-                send_back(m, k).wait_send()
-
-        @pl.when(is_first)
-        def _():
-            send_y(m).wait_send()
-            grad_own(m).wait()
-            grad_other(m).wait()
-
-    each(STEPS, drain)
-    for c in set_b() + set_f() + set_d() + set_g() + set_h():
-        c.wait_send()
-    sent_sibs()
-    fix.wait_send()
-    keep_own.wait()
+        drain_last()
+
+    fix.wait()
+    drain_step(STEPS - 1)
 
 
 def run_window(weight, acts, gates, out_grad):

time: 114 us -> 113 us (level)
  Pallas kernels: 114 us -> 112 us
    pallas_call x1, Pallas kernels: 103 us -> 101 us  [run_window(): pl.pallas_call(window_kernel, out_shape=(pltpu.VMEM((tokens, width), BF),...]
where the time goes in v5:
time: 113 us
  Pallas kernels  112 us (99%)
    pallas_call x1, Pallas kernels, run_window(): pl.pallas_call(window_kernel, out_shape=(pltpu.VMEM((tokens, width), BF),...  101 us
    pallas_call x1, Pallas kernels, run_owned(): pl.pallas_call(owned_kernel, out_shape=(jax.ShapeDtypeStruct((cap, width)...  10.8 us

profile of v5, /device:TPU:1, one launch (start us, length us, event | category | flops | bytes accessed | tf_op | source)
XLA Modules:
  0.0 112.5 jit_solution(7850171378356734185)
XLA Ops:
  0.6 0.0 copy-start
  0.6 101.1 %window.1 = (bf16[256,1024]{1,0:T(8,128)(2,1)S(1)}, bf16[2,2,4,2,256,1024]{5,4,3,2,1,0:T(8,128)(2,1)}, bf16[2,2,256,1024]{3,2,1,0:T(8,128)(2,1)S(1)}) custom-call(bf16[8192,1024]{1,0:T(8,128)(2,1)} %bitcast.6, bf16[256,1024]{1,0:T(8,128)(2,1)} %bitcast.7, bf16[256,1024]{1,0:T(8,128)(2,1)} %bitcast.8, bf16[256,1024]{1,0:T(8,128)(2,1)} %bitcast.9), custom_call_target="tpu_custom_call" | custom-call | flops 4294967296 | bytes 16777216 | tf_op jit(solution)/shard_map/window/pallas_call | solution.py:567
  101.7 0.0 copy-done
  101.7 10.8 %owned.1 = (bf16[3072,1024]{1,0:T(8,128)(2,1)}, bf16[256,1024]{1,0:T(8,128)(2,1)}) custom-call(s32[4,4]{1,0:T(4,128)S(1)} %copy-done, bf16[2,2,4,2,256,1024]{5,4,3,2,1,0:T(8,128)(2,1)} %get-tuple-element.7.acts, bf16[2,2,256,1024]{3,2,1,0:T(8,128)(2,1)S(1)} %get-tuple-element.8.pre, bf16[256,1024]{1,0:T(8,128)(2,1)S(1)} %get-tuple-element.9.grads), custom_call_target="tpu_custom_call" | custom-call | flops 6442450944 | bytes 37748736 | tf_op jit(solution)/shard_map/owned/pallas_call | solution.py:668
Async XLA Ops:
  0.6 101.1 %copy-start = (s32[4,4]{1,0:T(4,128)S(1)}, s32[4,4]{1,0:T(4,128)}, u32[]{:S(2)}) copy-start(s32[4,4]{1,0:T(4,128)} %owners.1) | copy-start | bytes 196
